TPU v7x, 32 devices: a whole 2x2x4 slice. The times are simulated.
32 devices in a mesh: dp: 2 (over y), head: 2 (over core), tile: 8 (over z, x).
Axes of the slice: x: 2, y: 2, z: 4, core: 2. Of those that a mesh axis runs over, the one named last changes fastest.
Arguments:
- tiles_in: bfloat16 [2, 2048, 2560], P('dp', 'tile'), may hold values from -6 to 6
- key_weight: bfloat16 [2560, 1280], P('tile', 'head'), may hold values from -0.125 to 0.125
- value_weight: bfloat16 [2560, 1280], P('tile', 'head'), may hold values from -0.125 to 0.125
- queries: bfloat16 [512, 1280], P(None, 'head'), may hold values from -300 to 300
- out_grad: bfloat16 [2, 512, 1280], P('dp', None, 'head'), may hold values from -192 to 192
- valid_count: int32 [2], P('dp'), may hold values from 512 to 2048, as said below
- tile_mask: int32 [2, 2048], P('dp', 'tile'), may hold values 0 or 1
Outputs:
- tile_grad: bfloat16 [2, 2048, 2560], P('dp', 'tile', 'head')
Inputs may be any that keep to these rules, and one draw needn't show every extreme that they name: Some slide has valid_count equal to 2048.
All inputs are finite; a program needn't handle non-finite values. No bound on the sum of `tile_mask` on one device may be relied on, other than what follows from the above.
Results may differ from a plain program's by a relative error of at most 0.022.
Values may be sent and summed in bfloat16 or wider, within the bound.
A program may use at most 64 MiB of HBM per device.

v0:
```python
import jax
import jax.numpy as jnp
from jax import lax
from jax.sharding import PartitionSpec as P

HDIM = 80


NEG_LARGE = -1e30


def per_device(tiles_in, key_weight, value_weight, queries, out_grad, valid_count, tile_mask):
    inv_scale = HDIM ** (-0.5)
    tile_dev = tiles_in.shape[1]
    group_width = queries.shape[1]
    heads_here = group_width // HDIM
    latents = queries.shape[0]
    local_tiles = tiles_in[0]
    positions = lax.axis_index("tile") * tile_dev + jnp.arange(tile_dev, dtype=jnp.int32)
    kept = (tile_mask[0] == 1) | (positions == 0)
    valid = ((positions < valid_count[0]) & kept)[None, None, :]
    full_key, full_value = (
        lax.all_gather(key_weight, "tile", axis=0, tiled=True),
        lax.all_gather(value_weight, "tile", axis=0, tiled=True),
    )
    keys = jnp.dot(local_tiles, full_key, preferred_element_type=jnp.float32)
    values = jnp.dot(local_tiles, full_value, preferred_element_type=jnp.float32).astype(
        jnp.bfloat16
    )
    query_heads = queries.reshape(latents, heads_here, HDIM)
    query_wide = queries.astype(jnp.float32).reshape(latents, heads_here, HDIM)
    key_heads = keys.reshape(tile_dev, heads_here, HDIM)
    value_heads = values.reshape(tile_dev, heads_here, HDIM)
    grad_heads = out_grad[0].reshape(latents, heads_here, HDIM)
    scores = (
        jnp.einsum(
            "lhd,thd->hlt",
            query_wide,
            key_heads,
            precision=lax.Precision.HIGHEST,
            preferred_element_type=jnp.float32,
        )
        * inv_scale
    )
    prob_grad = jnp.einsum(
        "lhd,thd->hlt", grad_heads, value_heads, preferred_element_type=jnp.float32
    )
    local_max = jnp.max(jnp.where(valid, scores, NEG_LARGE), axis=2)
    row_max = lax.pmax(local_max, "tile")
    expd = jnp.where(valid, jnp.exp(scores - row_max[:, :, None]), 0.0)
    total, weighted = lax.psum((jnp.sum(expd, axis=2), jnp.sum(expd * prob_grad, axis=2)), "tile")
    delta = weighted / total
    probs = expd / total[:, :, None]
    dscore = (inv_scale * probs * (prob_grad - delta[:, :, None])).astype(jnp.bfloat16)
    value_grad = (
        jnp.einsum(
            "hlt,lhd->thd",
            probs.astype(jnp.bfloat16),
            grad_heads,
            preferred_element_type=jnp.float32,
        )
        .astype(jnp.bfloat16)
        .reshape(tile_dev, group_width)
    )
    key_grad = (
        jnp.einsum("hlt,lhd->thd", dscore, query_heads, preferred_element_type=jnp.float32)
        .astype(jnp.bfloat16)
        .reshape(tile_dev, group_width)
    )
    partial_sum = jnp.einsum("tc,rc->tr", key_grad, full_key, preferred_element_type=jnp.float32)
    partial_sum = partial_sum + jnp.einsum(
        "tc,rc->tr", value_grad, full_value, preferred_element_type=jnp.float32
    )
    rounded = partial_sum.astype(jnp.bfloat16)
    summed = lax.psum_scatter(rounded[None], "head", scatter_dimension=2, tiled=True).astype(
        jnp.float32
    )
    return summed.astype(jnp.bfloat16)


def solution(mesh):
    return jax.shard_map(
        per_device,
        mesh=mesh,
        in_specs=(
            P("dp", "tile", None),
            P("tile", "head"),
            P("tile", "head"),
            P(None, "head"),
            P("dp", None, "head"),
            P("dp"),
            P("dp", "tile"),
        ),
        out_specs=P("dp", "tile", "head"),
        check_vma=False,
    )
```

profile of v0, /device:TPU:0, one launch (start us, length us, event | category | flops | bytes accessed | tf_op | source)
XLA Modules:
  0.0 246.7 jit_solution(2373447565799668983)
XLA Ops:
  6.5 0.0 copy-start
  6.5 0.0 all-gather.5.cloned.1.call-start
  6.5 0.7 all-gather.5.cloned.1.call-update
  7.3 0.0 all-gather.3.cloned.1.call-start
  7.3 0.7 all-gather.3.cloned.1.call-update
  8.0 0.0 reduce-scatter.2.cloned.1.call-start
  8.7 1.3 copy.22
  10.0 1.3 copy.24
  11.4 0.7 compare_reduce_fusion
  12.1 62.2 %all-gather.5.cloned.1.call-done = bf16[2560,640]{1,0:T(8,128)(2,1)} async-done(((bf16[320,640]{1,0:T(8,128)(2,1)}), bf16[2560,640]{1,0:T(8,128)(2,1)}) %all-gather.5.cloned.1.call-update) | async-done | bytes 3276816 | tf_op jit(solution)/shard_map/all_gather | solution.py:24
  74.2 0.0 copy-done
  74.2 3.1 %fusion.15 = bf16[256,640]{1,0:T(8,128)(2,1)S(1)} fusion(bf16[2560,640]{1,0:T(8,128)(2,1)} %all-gather.5.cloned.1.call-done, bf16[1,256,2560]{2,1,0:T(8,128)(2,1)S(1)} %copy-done), kind=kOutput, calls=%fused_computation.21 | convolution fusion | flops 839024640 | bytes 4915200 | tf_op jit(solution)/shard_map/dot_general | solution.py:27
  77.4 0.2 copy.23
  77.5 59.5 %all-gather.3.cloned.1.call-done = bf16[2560,640]{1,0:T(8,128)(2,1)} async-done(((bf16[320,640]{1,0:T(8,128)(2,1)}), bf16[2560,640]{1,0:T(8,128)(2,1)}) %all-gather.3.cloned.1.call-update) | async-done | bytes 3276816 | tf_op jit(solution)/shard_map/all_gather | solution.py:23
  137.0 5.7 %copy.21 = bf16[2560,640]{0,1:T(8,128)(2,1)} copy(bf16[2560,640]{1,0:T(8,128)(2,1)} %all-gather.3.cloned.1.call-done) | data formatting | bytes 6553600 | tf_op jit(solution)/shard_map/all_gather | solution.py:23
  142.7 3.0 %fusion.11 = f32[256,8,80]{0,2,1:T(8,128)S(1)} fusion(bf16[8,80,2560]{2,1,0:T(8,128)(2,1)} %bitcast.58, bf16[1,256,2560]{2,1,0:T(8,128)(2,1)S(1)} %copy-done), kind=kOutput, calls=%fused_computation.17 | convolution fusion | flops 838860800 | bytes 5242880 | tf_op jit(solution)/shard_map/dot_general | solution.py:26
  145.7 4.2 %select_reduce_fusion = (f32[8,512]{1,0:T(8,128)S(1)}, f32[8,256,512]{2,1,0:T(8,128)}) fusion(pred[256]{0:T(512)(128)(4,1)S(1)} %or_and_fusion, f32[256,8,80]{0,2,1:T(8,128)S(1)} %fusion.11, bf16[512,8,80]{0,2,1:T(8,128)(2,1)S(1)} %bitcast.61), kind=kOutput, calls=%fused_computation.8 | convolution fusion | flops 1009774592 | bytes 5521664 | tf_op jit(solution)/shard_map/lhd,thd->hlt/dot_general | solution.py:36
  149.8 34.7 %pmax.7 = f32[8,512]{1,0:T(8,128)S(1)} all-reduce(f32[8,512]{1,0:T(8,128)S(1)} %get-tuple-element.9), channel_id=1, replica_groups=mesh['dp'=2,'head'=2,'tile'=8] {'tile'}, use_global_device_ids=true, to_apply=%region_1.2 | all-reduce | flops 4096 | bytes 32768 | tf_op jit(solution)/shard_map/pmax | solution.py:49
  184.6 5.7 %bitcast_reduce_fusion = (f32[8,512]{1,0:T(8,128)S(1)}, f32[8,512]{1,0:T(8,128)S(1)}, f32[8,256,512]{2,1,0:T(8,128)}) fusion(f32[8,256,512]{2,1,0:T(8,128)} %get-tuple-element.10, f32[8,512]{1,0:T(8,128)S(1)} %pmax.7, pred[256]{0:T(512)(128)(4,1)S(1)} %or_and_fusion, bf16[256,8,80]{0,2,1:T(8,128)(2,1)S(1)} %bitcast.63, bf16[512,8,80]{0,2,1:T(8,128)(2,1)S(1)} %bitcast.59), kind=kOutput, calls=%fused_computation.6 | convolution fusion | flops 174055424 | bytes 9421056 | tf_op jit(solution)/shard_map/lhd,thd->hlt/dot_general | solution.py:45
  190.3 33.0 %all-reduce = (f32[8,512]{1,0:T(8,128)S(1)}, f32[8,512]{1,0:T(8,128)S(1)}) all-reduce(f32[8,512]{1,0:T(8,128)S(1)} %get-tuple-element.6, f32[8,512]{1,0:T(8,128)S(1)} %get-tuple-element.5), channel_id=1, replica_groups=mesh['dp'=2,'head'=2,'tile'=8] {'tile'}, use_global_device_ids=true, to_apply=%region_5.6 | all-reduce | flops 8192 | bytes 65536 | tf_op jit(solution)/shard_map/psum | solution.py:51
  223.3 0.0 copy-start.1
  223.3 0.0 copy-start.3
  223.3 3.5 %fusion.18 = bf16[8,256,80]{1,2,0:T(8,128)(2,1)S(1)} fusion(bf16[512,8,80]{0,2,1:T(8,128)(2,1)S(1)} %bitcast.60, f32[8,256,512]{2,1,0:T(8,128)} %get-tuple-element.10, f32[8,512]{1,0:T(8,128)S(1)} %get-tuple-element.8, f32[8,512]{1,0:T(8,128)S(1)} %pmax.7, pred[256]{0:T(512)(128)(4,1)S(1)} %or_and_fusion), kind=kOutput, calls=%fused_computation.22 | convolution fusion | flops 173178880 | bytes 5210368 | tf_op jit(solution)/shard_map/hlt,lhd->thd/dot_general | solution.py:56
  226.8 0.0 copy-done.1
  226.8 1.2 copy-done.3
  228.0 0.0 copy-start.2
  228.0 1.6 fusion.21
  229.6 0.0 copy-start.4
  229.6 0.4 copy-done.2
  229.9 1.2 fusion.25
  231.2 0.4 copy-done.4
  231.6 2.4 fusion.4
  234.0 0.0 reduce-scatter.2.cloned.1.call-update
  234.0 6.2 %reduce-scatter.2.cloned.1.call-done = bf16[1,256,1280]{2,1,0:T(8,128)(2,1)} async-done(((bf16[1,256,2560]{2,1,0:T(8,128)(2,1)}), bf16[1,256,1280]{2,1,0:T(8,128)(2,1)}) %reduce-scatter.2.cloned.1.call-update) | async-done | bytes 655376 | tf_op jit(solution)/shard_map/reduce_scatter | solution.py:75
  (2 shorter events, 0.0 us)
Async XLA Ops:
  6.5 67.7 %copy-start = (bf16[1,256,2560]{2,1,0:T(8,128)(2,1)S(1)}, bf16[1,256,2560]{2,1,0:T(8,128)(2,1)}, u32[]{:S(2)}) copy-start(bf16[1,256,2560]{2,1,0:T(8,128)(2,1)} %param.7) | copy-start | bytes 3932164
  6.5 67.7 %all-gather.5.cloned.1.call-start = ((), (), s32[]{:S(2)}) async-start(), calls=%async_computation.2 | async-start | bytes 3686400 | tf_op jit(solution)/shard_map/all_gather | solution.py:24
  7.3 129.8 %all-gather.3.cloned.1.call-start = ((), (), s32[]{:S(2)}) async-start(), calls=%async_computation.1 | async-start | bytes 3686400 | tf_op jit(solution)/shard_map/all_gather | solution.py:23
  8.0 232.1 %reduce-scatter.2.cloned.1.call-start = ((), (), s32[]{:S(2)}) async-start(), calls=%async_computation.3 | async-start | bytes 1966080 | tf_op jit(solution)/shard_map/reduce_scatter | solution.py:75
  223.3 3.5 %copy-start.1 = (f32[8,256,512]{2,1,0:T(8,128)S(1)}, f32[8,256,512]{2,1,0:T(8,128)}, u32[]{:S(2)}) copy-start(f32[8,256,512]{2,1,0:T(8,128)} %get-tuple-element.10) | copy-start | bytes 12582916
  223.3 4.7 %copy-start.3 = (f32[8,256,512]{2,1,0:T(8,128)S(1)}, f32[8,256,512]{2,1,0:T(8,128)}, u32[]{:S(2)}) copy-start(f32[8,256,512]{2,1,0:T(8,128)} %get-tuple-element.11) | copy-start | bytes 12582916
  228.0 1.9 copy-start.2
  229.6 2.0 copy-start.4
Sparse Core Ops, SparseCore 0:
  9.5 64.6 all-gather.4
  76.4 60.5 all-gather.2
  234.1 5.9 reduce-scatter.1
where the time goes:
time: 247 us
  waiting for transfers between devices  129 us (52%)
  blocking collectives  67.8 us (27%)
  matrix products  24.5 us (10%)
  between operations  13.8 us (6%)
  local copies, waits for them, and re-layouts  10.5 us (4%)
    all_gather x1, waiting for transfers between devices, per_device(): lax.all_gather(value_weight, 'tile', axis=0, tiled=True)  62.2 us
    all_gather x1, waiting for transfers between devices, per_device(): lax.all_gather(key_weight, 'tile', axis=0, tiled=True)  59.5 us
    pmax x1, blocking collectives, per_device(): row_max = lax.pmax(local_max, 'tile')  34.7 us
    psum x1, blocking collectives, per_device(): lax.psum((jnp.sum(expd, axis=2), jnp.sum(expd * prob_grad, axis=2)), 'tile')  33 us
    reduce_scatter x1, waiting for transfers between devices, per_device(): lax.psum_scatter(rounded[None], 'head', scatter_dimension=2, tiled=True)  6.15 us
    dot_general x1, matrix products, per_device(): jnp.einsum('lhd,thd->hlt', grad_heads, value_heads, preferred_element_typ...  5.69 us
    all_gather x1, local copies, waits for them, and re-layouts, per_device(): lax.all_gather(key_weight, 'tile', axis=0, tiled=True)  5.68 us
  transfers between devices with their start and end apart: 3, of which 3 were waited for; matrix products, arithmetic and copies ran while one was open for 3% of the time, Pallas kernels for 0%

commit v1 on v0

--- a/solution.py
+++ b/solution.py
@@ -1,12 +1,20 @@
+import functools
+
 import jax
 import jax.numpy as jnp
 from jax import lax
+from jax.experimental import pallas as pl
+from jax.experimental.pallas import tpu as pltpu
 from jax.sharding import PartitionSpec as P
 
 HDIM = 80
 
 
 NEG_LARGE = -1e30
+NEG_FLOOR = -1e29
+WIN = 256
+UP, DOWN, ACROSS, TWIN = range(4)
+MESH = pl.DeviceIdType.MESH
 
 
 def per_device(tiles_in, key_weight, value_weight, queries, out_grad, valid_count, tile_mask):
@@ -78,9 +86,390 @@
     return summed.astype(jnp.bfloat16)
 
 
+def dot_nt(a, b):
+    return lax.dot_general(a, b, (((1,), (1,)), ((), ())), preferred_element_type=jnp.float32)
+
+
+def dot_nn(a, b):
+    return jnp.dot(a, b, preferred_element_type=jnp.float32)
+
+
+def fused(
+    line, across, shard, width, heads, chunks,
+    tiles_hbm, key_hbm, value_hbm, query_hbm, grad_hbm, valid_ref,
+    out_ref,
+    weights, tiles, query, grad, query_win, grad_win, key_parts, values, expd, prob_grad,
+    max_buf, lse_all, weighted_all, row_buf, value_grad, key_grad, acc, to_pair, from_pair,
+    local_sem, send_sem, recv_sem, lse_send, lse_recv, sum_send, sum_recv, pair_send, pair_recv,
+):
+    n_tile = line * across
+    half = shard // 2
+    inv_scale = HDIM ** (-0.5)
+    me = lax.axis_index("tile")
+    slide = lax.axis_index("dp")
+    group = lax.axis_index("head")
+    z = me // across
+    x = me % across
+    beside = me + 1 - 2 * x
+    twin = slide + 1 - 2 * (slide % 2)
+    mine, other = slide % 2, 1 - slide % 2
+    devices = {
+        UP: {"tile": me + across},
+        DOWN: {"tile": me - across},
+        ACROSS: {"tile": beside},
+        TWIN: {"dp": twin},
+    }
+    sources = (key_hbm, value_hbm)
+    started = []
+
+    def copy_in(src, dst, index):
+        copy = pltpu.make_async_copy(src, dst, local_sem.at[index])
+        copy.start()
+        return copy
+
+    own_rows = pl.ds(pl.multiple_of(me * shard, 16), shard)
+    query_copy = copy_in(query_hbm, query, 0)
+    grad_copy = copy_in(grad_hbm.at[0], grad, 1)
+    tiles_copy = copy_in(tiles_hbm.at[0], tiles, 2)
+    own_copies = [copy_in(sources[m], weights.at[m, own_rows], 3 + m) for m in range(2)]
+
+    barrier = pltpu.get_barrier_semaphore()
+    for step in range(1, n_tile):
+        pl.semaphore_signal(
+            barrier, inc=1, device_id={"tile": (me + step) % n_tile}, device_id_type=MESH
+        )
+    pl.semaphore_signal(barrier, inc=1, device_id={"dp": twin}, device_id_type=MESH)
+    pl.semaphore_signal(barrier, inc=1, device_id={"head": 1 - group}, device_id_type=MESH)
+    pl.semaphore_wait(barrier, n_tile + 1)
+
+    def piece(m, owner, part, way, first=False):
+        rows = pl.ds(pl.multiple_of(owner * shard + part * half, 16), half)
+        src = weights.at[m, rows]
+        if first:
+            src = sources[m].at[pl.ds(pl.multiple_of(part * half, 16), half)]
+        index = ((m * n_tile + owner) * 2 + part) * 4 + way
+        return pltpu.make_async_remote_copy(
+            src_ref=src,
+            dst_ref=weights.at[m, rows],
+            send_sem=send_sem.at[index],
+            recv_sem=recv_sem.at[(m * n_tile + owner) * 2 + part],
+            device_id=devices[way],
+            device_id_type=MESH,
+        )
+
+    def send(cond, *what):
+        if cond is None:
+            piece(*what).start()
+        else:
+            pl.when(cond)(lambda: piece(*what).start())
+        started.append((cond, what))
+
+    def arrive(cond, m, owner, part):
+        if cond is None:
+            piece(m, owner, part, ACROSS).wait_recv()
+        else:
+            pl.when(cond)(lambda: piece(m, owner, part, ACROSS).wait_recv())
+
+    def both(a, b):
+        return b if a is None else (a if b is None else jnp.logical_and(a, b))
+
+    can_up, can_down = z < line - 1, z > 0
+
+    def open_round(m):
+        send(can_up, m, me, mine, UP, True)
+        send(can_down, m, me, mine, DOWN, True)
+        send(None, m, me, mine, ACROSS, True)
+        send(can_up, m, me, other, UP, True)
+        send(can_down, m, me, other, DOWN, True)
+
+    def held_at(base, distance):
+        if distance == 0:
+            return [(None, base)]
+        return [
+            (z >= distance, base - distance * across),
+            (z + distance < line, base + distance * across),
+        ]
+
+    def side_round(m, distance):
+        for there, owner in held_at(beside, distance):
+            arrive(there, m, owner, mine)
+            send(there, m, owner, mine, TWIN)
+
+    def line_round(m, distance):
+        last = distance == line - 1
+        ways = ((UP, can_up), (DOWN, can_down))
+        for (there, owner), (way, can) in zip(held_at(me, distance), ways):
+            arrive(there, m, owner, mine)
+            if not last:
+                send(both(there, can), m, owner, mine, way)
+            send(there, m, owner, mine, ACROSS)
+            if last:
+                send(there, m, owner, mine, TWIN)
+        if not last:
+            for (there, owner), (way, can) in zip(held_at(me, distance), ways):
+                arrive(there, m, owner, other)
+                if distance + 1 < line - 1:
+                    send(both(there, can), m, owner, other, way)
+        side_round(m, distance - 1)
+
+    def close_round(m):
+        side_round(m, line - 1)
+        for distance in range(line):
+            for there, owner in held_at(beside, distance):
+                arrive(there, m, owner, other)
+        for there, owner in held_at(me, line - 1):
+            arrive(there, m, owner, other)
+
+    def window(head):
+        start = 128 * jnp.minimum((head * HDIM) // 128, (width - WIN) // 128)
+        return pl.multiple_of(start, 128)
+
+    def spread(buffer, send_sems, recv_sems):
+        copies = []
+        for step in range(1, n_tile):
+            copies.append(
+                pltpu.make_async_remote_copy(
+                    src_ref=buffer.at[me],
+                    dst_ref=buffer.at[me],
+                    send_sem=send_sems.at[step],
+                    recv_sem=recv_sems.at[me],
+                    device_id={"tile": (me + step) % n_tile},
+                    device_id_type=MESH,
+                )
+            )
+            copies[-1].start()
+        return copies
+
+    def collect(buffer, send_sems, recv_sems):
+        for step in range(1, n_tile):
+            owner = (me + n_tile - step) % n_tile
+            pltpu.make_async_remote_copy(
+                src_ref=buffer.at[owner],
+                dst_ref=buffer.at[owner],
+                send_sem=send_sems.at[step],
+                recv_sem=recv_sems.at[owner],
+                device_id={"tile": owner},
+                device_id_type=MESH,
+            ).wait_recv()
+
+    open_round(0)
+
+    query_copy.wait()
+    grad_copy.wait()
+
+    @pl.loop(0, heads)
+    def _(head):
+        start = window(head)
+        column = start + lax.broadcasted_iota(jnp.int32, (query.shape[0], WIN), 1)
+        inside = (column >= head * HDIM) & (column < (head + 1) * HDIM)
+        for whole, cut in ((query, query_win), (grad, grad_win)):
+            part = whole[:, pl.ds(start, WIN)].astype(jnp.float32)
+            cut[head] = jnp.where(inside, part, 0.0).astype(jnp.bfloat16)
+
+    value_grad[...] = jnp.zeros_like(value_grad)
+    key_grad[...] = jnp.zeros_like(key_grad)
+
+    line_round(0, 1)
+    for distance in range(2, line):
+        line_round(0, distance)
+        if distance == 2:
+            open_round(1)
+    close_round(0)
+
+    tiles_copy.wait()
+    for copy in own_copies:
+        copy.wait()
+    keys = dot_nn(tiles[...], weights[0])
+    for index in range(3):
+        part = keys.astype(jnp.bfloat16)
+        key_parts[index] = part
+        keys = keys - part.astype(jnp.float32)
+
+    line_round(1, 1)
+
+    @pl.loop(0, heads)
+    def _(head):
+        start = window(head)
+        cut = query_win[head]
+        scores = dot_nt(key_parts[2, :, pl.ds(start, WIN)], cut)
+        scores = scores + dot_nt(key_parts[1, :, pl.ds(start, WIN)], cut)
+        scores = scores + dot_nt(key_parts[0, :, pl.ds(start, WIN)], cut)
+        scores = jnp.where(valid_ref[...] > 0.0, scores * inv_scale, NEG_LARGE)
+        row_max = jnp.maximum(jnp.max(scores, axis=0, keepdims=True), NEG_FLOOR)
+        powers = jnp.exp(scores - row_max)
+        total = jnp.sum(powers, axis=0, keepdims=True)
+        expd[head] = powers
+        max_buf[pl.ds(head, 1), :] = row_max
+        lse_all[me, pl.ds(head, 1), :] = row_max + jnp.log(jnp.maximum(total, 1e-37))
+
+    lse_copies = spread(lse_all, lse_send, lse_recv)
+    for distance in range(2, line):
+        line_round(1, distance)
+    collect(lse_all, lse_send, lse_recv)
+    top = lse_all[0]
+    for index in range(1, n_tile):
+        top = jnp.maximum(top, lse_all[index])
+    total = jnp.exp(lse_all[0] - top)
+    for index in range(1, n_tile):
+        total = total + jnp.exp(lse_all[index] - top)
+    row_buf[...] = jnp.exp(max_buf[...] - (top + jnp.log(total)))
+
+    @pl.loop(0, heads)
+    def _(head):
+        expd[head] = expd[head] * row_buf[pl.ds(head, 1), :]
+
+    @pl.loop(0, heads)
+    def _(head):
+        start = window(head)
+        value_grad[:, pl.ds(start, WIN)] += dot_nn(expd[head].astype(jnp.bfloat16), grad_win[head])
+
+    close_round(1)
+
+    values[...] = dot_nn(tiles[...], weights[1]).astype(jnp.bfloat16)
+
+    @pl.loop(0, heads)
+    def _(head):
+        start = window(head)
+        part = dot_nt(values[:, pl.ds(start, WIN)], grad_win[head])
+        prob_grad[head] = part
+        weighted_all[me, pl.ds(head, 1), :] = jnp.sum(expd[head] * part, axis=0, keepdims=True)
+
+    sum_copies = spread(weighted_all, sum_send, sum_recv)
+
+    value_cast = value_grad[...].astype(jnp.bfloat16)
+
+    @pl.loop(0, 2 * chunks)
+    def _(index):
+        rows = pl.ds(pl.multiple_of(index * WIN, WIN), WIN)
+        acc[index] = dot_nt(value_cast, weights[1, rows, :])
+
+    collect(weighted_all, sum_send, sum_recv)
+    delta = weighted_all[0]
+    for index in range(1, n_tile):
+        delta = delta + weighted_all[index]
+    row_buf[...] = delta
+
+    @pl.loop(0, heads)
+    def _(head):
+        start = window(head)
+        gap = prob_grad[head] - row_buf[pl.ds(head, 1), :]
+        dscore = (inv_scale * expd[head] * gap).astype(jnp.bfloat16)
+        key_grad[:, pl.ds(start, WIN)] += dot_nn(dscore, query_win[head])
+
+    key_cast = key_grad[...].astype(jnp.bfloat16)
+
+    def pair_copy(index):
+        return pltpu.make_async_remote_copy(
+            src_ref=to_pair.at[index],
+            dst_ref=from_pair.at[index],
+            send_sem=pair_send.at[index],
+            recv_sem=pair_recv.at[index],
+            device_id={"head": 1 - group},
+            device_id_type=MESH,
+        )
+
+    @pl.loop(0, chunks)
+    def _(index):
+        chunk = chunks * (1 - group) + index
+        rows = pl.ds(pl.multiple_of(chunk * WIN, WIN), WIN)
+        to_pair[index] = (acc[chunk] + dot_nt(key_cast, weights[0, rows, :])).astype(jnp.bfloat16)
+        pair_copy(index).start()
+
+    @pl.loop(0, chunks)
+    def _(index):
+        chunk = chunks * group + index
+        rows = pl.ds(pl.multiple_of(chunk * WIN, WIN), WIN)
+        acc[chunk] += dot_nt(key_cast, weights[0, rows, :])
+
+    for index in range(chunks):
+        pair_copy(index).wait_recv()
+        total = acc[chunks * group + index] + from_pair[index].astype(jnp.float32)
+        out_ref[0, :, index * WIN : (index + 1) * WIN] = total.astype(jnp.bfloat16)
+
+    for index in range(chunks):
+        pair_copy(index).wait_send()
+    for copy in lse_copies + sum_copies:
+        copy.wait_send()
+    for cond, what in started:
+        if cond is None:
+            piece(*what).wait_send()
+        else:
+            pl.when(cond)(functools.partial(lambda w: piece(*w).wait_send(), what))
+
+
+def fused_device(across, tiles_in, key_weight, value_weight, queries, out_grad, valid_count, tile_mask):
+    n_tile = lax.axis_size("tile")
+    tile_dev, depth = tiles_in.shape[1:]
+    latents, width = queries.shape
+    shard = key_weight.shape[0]
+    heads = width // HDIM
+    chunks = depth // 2 // WIN
+    positions = lax.axis_index("tile") * tile_dev + jnp.arange(tile_dev, dtype=jnp.int32)
+    kept = (tile_mask[0] == 1) | (positions == 0)
+    valid = ((positions < valid_count[0]) & kept).astype(jnp.float32)[:, None]
+    bf16, f32 = jnp.bfloat16, jnp.float32
+    dma = pltpu.SemaphoreType.DMA
+    return pl.pallas_call(
+        functools.partial(fused, n_tile // across, across, shard, width, heads, chunks),
+        out_shape=jax.ShapeDtypeStruct((1, tile_dev, depth // 2), bf16),
+        in_specs=[pl.BlockSpec(memory_space=pl.ANY)] * 5
+        + [pl.BlockSpec(memory_space=pltpu.VMEM)],
+        out_specs=pl.BlockSpec(memory_space=pltpu.VMEM),
+        scratch_shapes=[
+            pltpu.VMEM((2, depth, width), bf16),
+            pltpu.VMEM((tile_dev, depth), bf16),
+            pltpu.VMEM((latents, width), bf16),
+            pltpu.VMEM((latents, width), bf16),
+            pltpu.VMEM((heads, latents, WIN), bf16),
+            pltpu.VMEM((heads, latents, WIN), bf16),
+            pltpu.VMEM((3, tile_dev, width), bf16),
+            pltpu.VMEM((tile_dev, width), bf16),
+            pltpu.VMEM((heads, tile_dev, latents), f32),
+            pltpu.VMEM((heads, tile_dev, latents), f32),
+            pltpu.VMEM((heads, latents), f32),
+            pltpu.VMEM((n_tile, heads, latents), f32),
+            pltpu.VMEM((n_tile, heads, latents), f32),
+            pltpu.VMEM((heads, latents), f32),
+            pltpu.VMEM((tile_dev, width), f32),
+            pltpu.VMEM((tile_dev, width), f32),
+            pltpu.VMEM((2 * chunks, tile_dev, WIN), f32),
+            pltpu.VMEM((chunks, tile_dev, WIN), bf16),
+            pltpu.VMEM((chunks, tile_dev, WIN), bf16),
+            dma((5,)),
+            dma((2 * n_tile * 2 * 4,)),
+            dma((2 * n_tile * 2,)),
+            dma((n_tile,)),
+            dma((n_tile,)),
+            dma((n_tile,)),
+            dma((n_tile,)),
+            dma((chunks,)),
+            dma((chunks,)),
+        ],
+        compiler_params=pltpu.CompilerParams(
+            collective_id=0, has_side_effects=True, vmem_limit_bytes=56 * 2**20
+        ),
+        cost_estimate=pl.CostEstimate(
+            flops=4 * tile_dev * depth * width * 2, bytes_accessed=8 * 2**20, transcendentals=2**20
+        ),
+    )(tiles_in, key_weight, value_weight, queries, out_grad, valid)
+
+
 def solution(mesh):
+    across = mesh.shape["dp"]
+
+    def device(tiles_in, key_weight, *rest):
+        fits = (
+            across == 2
+            and mesh.shape["head"] == 2
+            and mesh.shape["tile"] >= 3 * across
+            and key_weight.shape[0] % 32 == 0
+            and tiles_in.shape[2] % (2 * WIN) == 0
+        )
+        body = functools.partial(fused_device, across) if fits else per_device
+        return body(tiles_in, key_weight, *rest)
+
     return jax.shard_map(
-        per_device,
+        device,
         mesh=mesh,
         in_specs=(
             P("dp", "tile", None),

time: 247 us -> 90.2 us (0.37)
  waiting for transfers between devices: 129 us -> 0 us
  Pallas kernels: 0 us -> 85.8 us
  blocking collectives: 67.8 us -> 0 us
  matrix products: 24.5 us -> 0 us
  between operations: 13.8 us -> 0.67 us
  local copies, waits for them, and re-layouts: 10.5 us -> 2.14 us
    all_gather x2 -> x0, waiting for transfers between devices: 122 us -> none  [the longest x1 62.2 us: per_device(): lax.all_gather(value_weight, 'tile', axis=0, tiled=True)]
    pallas_call x0 -> x1, Pallas kernels: none -> 85.8 us  [fused_device(): pl.pallas_call(functools.partial(fused, n_tile // across, across, shard,...]
    pmax x1 -> x0, blocking collectives: 34.7 us -> none  [per_device(): row_max = lax.pmax(local_max, 'tile')]
    psum x1 -> x0, blocking collectives: 33 us -> none  [per_device(): lax.psum((jnp.sum(expd, axis=2), jnp.sum(expd * prob_grad, axis=2)), 'tile')]
    dot_general x8 -> x0, matrix products: 24.5 us -> none  [the longest x1 5.69 us: per_device(): jnp.einsum('lhd,thd->hlt', grad_heads, value_heads, preferred_element_typ...]
    reduce_scatter x1 -> x0, waiting for transfers between devices: 6.15 us -> none  [per_device(): lax.psum_scatter(rounded[None], 'head', scatter_dimension=2, tiled=True)]
    all_gather x1 -> x0, local copies, waits for them, and re-layouts: 5.68 us -> none  [per_device(): lax.all_gather(key_weight, 'tile', axis=0, tiled=True)]
    unnamed x12 -> x1, local copies, waits for them, and re-layouts: 4.69 us -> 1.97 us
  transfers between devices with their start and end apart: 3 -> 0, of which waited for: 3 -> 0; matrix products, arithmetic and copies ran while one was open for 3% -> 0% of each run, Pallas kernels for 0% -> 0%
where the time goes in v1:
time: 90.2 us; the launch traced here: 90 us
  Pallas kernels  85.8 us (95%)
  local copies, waits for them, and re-layouts  2.14 us (2%)
  other arithmetic  1.39 us (2%)
    pallas_call x1, Pallas kernels, fused_device(): pl.pallas_call(functools.partial(fused, n_tile // across, across, shard,...  85.8 us
    unnamed x1, local copies, waits for them, and re-layouts  1.97 us

profile of v1, /device:TPU:0, one launch (start us, length us, event | category | flops | bytes accessed | tf_op | source)
XLA Modules:
  0.0 90.0 jit_solution(6485751633265451304)
XLA Ops:
  0.7 0.7 compare_bitcast_fusion
  1.3 0.2 copy.10
  1.5 0.7 fusion.3.valid_ref
  2.2 85.8 %shard_map.73 = bf16[1,256,1280]{2,1,0:T(8,128)(2,1)} custom-call(bf16[1,256,2560]{2,1,0:T(8,128)(2,1)} %tiles_hbm.1, bf16[320,640]{1,0:T(8,128)(2,1)} %key_hbm.1, bf16[320,640]{1,0:T(8,128)(2,1)} %value_hbm.1, bf16[512,640]{1,0:T(8,128)(2,1)} %query_hbm.1, bf16[1,512,640]{2,1,0:T(8,128)(2,1)} %grad_hbm.1, f32[256,1]{1,0:T(8,128)} %fusion.3.valid_ref), custom_call_target="tpu_custom_call" | custom-call | flops 3355443200 | bytes 8388608 | tf_op jit(solution)/shard_map/pallas_call | solution.py:412
  88.0 2.0 %copy.13 = bf16[1,256,1280]{2,1,0:T(8,128)(2,1)} copy(bf16[1,256,1280]{2,1,0:T(8,128)(2,1)} %shard_map.73) | data formatting | bytes 1310720

commit v2 on v1

--- a/solution.py
+++ b/solution.py
@@ -13,6 +13,8 @@
 NEG_LARGE = -1e30
 NEG_FLOOR = -1e29
 WIN = 256
+SUBS = 2
+SENDS = 192
 UP, DOWN, ACROSS, TWIN = range(4)
 MESH = pl.DeviceIdType.MESH
 
@@ -96,14 +98,15 @@
 
 def fused(
     line, across, shard, width, heads, chunks,
-    tiles_hbm, key_hbm, value_hbm, query_hbm, grad_hbm, valid_ref,
-    out_ref,
+    tiles_hbm, key_hbm, value_hbm, query_hbm, grad_hbm, count_ref, mask_ref,
+    own_ref, pair_ref,
     weights, tiles, query, grad, query_win, grad_win, key_parts, values, expd, prob_grad,
-    max_buf, lse_all, weighted_all, row_buf, value_grad, key_grad, acc, to_pair, from_pair,
+    max_buf, lse_all, weighted_all, row_buf, value_grad, key_grad, acc, to_pair, valid,
     local_sem, send_sem, recv_sem, lse_send, lse_recv, sum_send, sum_recv, pair_send, pair_recv,
 ):
     n_tile = line * across
     half = shard // 2
+    size = half // SUBS
     inv_scale = HDIM ** (-0.5)
     me = lax.axis_index("tile")
     slide = lax.axis_index("dp")
@@ -142,45 +145,44 @@
     pl.semaphore_signal(barrier, inc=1, device_id={"head": 1 - group}, device_id_type=MESH)
     pl.semaphore_wait(barrier, n_tile + 1)
 
-    def piece(m, owner, part, way, first=False):
-        rows = pl.ds(pl.multiple_of(owner * shard + part * half, 16), half)
+    def piece(m, owner, part, sub, way, first=False):
+        offset = part * half + sub * size
+        rows = pl.ds(pl.multiple_of(owner * shard + offset, 16), size)
         src = weights.at[m, rows]
         if first:
-            src = sources[m].at[pl.ds(pl.multiple_of(part * half, 16), half)]
-        index = ((m * n_tile + owner) * 2 + part) * 4 + way
+            src = sources[m].at[pl.ds(pl.multiple_of(offset, 16), size)]
+        return src, weights.at[m, rows], ((m * n_tile + owner) * 2 + part) * SUBS + sub, devices[way]
+
+    def remote(index, *what):
+        src, dst, landing, device = piece(*what)
         return pltpu.make_async_remote_copy(
             src_ref=src,
-            dst_ref=weights.at[m, rows],
+            dst_ref=dst,
             send_sem=send_sem.at[index],
-            recv_sem=recv_sem.at[(m * n_tile + owner) * 2 + part],
-            device_id=devices[way],
+            recv_sem=recv_sem.at[landing],
+            device_id=device,
             device_id_type=MESH,
         )
 
     def send(cond, *what):
+        index = len(started)
+        started.append((cond, what))
         if cond is None:
-            piece(*what).start()
+            remote(index, *what).start()
         else:
-            pl.when(cond)(lambda: piece(*what).start())
-        started.append((cond, what))
-
-    def arrive(cond, m, owner, part):
+            pl.when(cond)(lambda: remote(index, *what).start())
+
+    def arrive(cond, m, owner, part, sub):
         if cond is None:
-            piece(m, owner, part, ACROSS).wait_recv()
+            remote(0, m, owner, part, sub, ACROSS).wait_recv()
         else:
-            pl.when(cond)(lambda: piece(m, owner, part, ACROSS).wait_recv())
+            pl.when(cond)(lambda: remote(0, m, owner, part, sub, ACROSS).wait_recv())
 
     def both(a, b):
         return b if a is None else (a if b is None else jnp.logical_and(a, b))
 
     can_up, can_down = z < line - 1, z > 0
-
-    def open_round(m):
-        send(can_up, m, me, mine, UP, True)
-        send(can_down, m, me, mine, DOWN, True)
-        send(None, m, me, mine, ACROSS, True)
-        send(can_up, m, me, other, UP, True)
-        send(can_down, m, me, other, DOWN, True)
+    ways = ((UP, can_up), (DOWN, can_down))
 
     def held_at(base, distance):
         if distance == 0:
@@ -190,35 +192,48 @@
             (z + distance < line, base + distance * across),
         ]
 
+    def open_own(m):
+        for sub in range(SUBS):
+            for way, can in ways:
+                send(can, m, me, mine, sub, way, True)
+            send(None, m, me, mine, sub, ACROSS, True)
+
     def side_round(m, distance):
-        for there, owner in held_at(beside, distance):
-            arrive(there, m, owner, mine)
-            send(there, m, owner, mine, TWIN)
-
-    def line_round(m, distance):
+        for sub in range(SUBS):
+            for there, owner in held_at(beside, distance):
+                arrive(there, m, owner, mine, sub)
+                send(there, m, owner, mine, sub, TWIN)
+
+    def own_round(m, distance):
         last = distance == line - 1
-        ways = ((UP, can_up), (DOWN, can_down))
-        for (there, owner), (way, can) in zip(held_at(me, distance), ways):
-            arrive(there, m, owner, mine)
-            if not last:
-                send(both(there, can), m, owner, mine, way)
-            send(there, m, owner, mine, ACROSS)
-            if last:
-                send(there, m, owner, mine, TWIN)
-        if not last:
+        for sub in range(SUBS):
             for (there, owner), (way, can) in zip(held_at(me, distance), ways):
-                arrive(there, m, owner, other)
+                arrive(there, m, owner, mine, sub)
+                if not last:
+                    send(both(there, can), m, owner, mine, sub, way)
+                send(there, m, owner, mine, sub, ACROSS)
+                if last:
+                    send(there, m, owner, mine, sub, TWIN)
+        for way, can, ends in ((UP, can_up, z), (DOWN, can_down, line - 1 - z)):
+            turn = jnp.maximum(ends, 1) == distance
+            for sub in range(SUBS):
+                send(both(turn, can), m, me, other, sub, way, True)
+        side_round(m, distance - 1)
+
+    def other_round(m, distance):
+        for sub in range(SUBS):
+            for (there, owner), (way, can) in zip(held_at(me, distance), ways):
+                arrive(there, m, owner, other, sub)
                 if distance + 1 < line - 1:
-                    send(both(there, can), m, owner, other, way)
-        side_round(m, distance - 1)
+                    send(both(there, can), m, owner, other, sub, way)
 
     def close_round(m):
-        side_round(m, line - 1)
-        for distance in range(line):
-            for there, owner in held_at(beside, distance):
-                arrive(there, m, owner, other)
-        for there, owner in held_at(me, line - 1):
-            arrive(there, m, owner, other)
+        for sub in range(SUBS):
+            for distance in range(line):
+                for there, owner in held_at(beside, distance):
+                    arrive(there, m, owner, other, sub)
+            for there, owner in held_at(me, line - 1):
+                arrive(there, m, owner, other, sub)
 
     def window(head):
         start = 128 * jnp.minimum((head * HDIM) // 128, (width - WIN) // 128)
@@ -252,7 +267,11 @@
                 device_id_type=MESH,
             ).wait_recv()
 
-    open_round(0)
+    open_own(0)
+
+    positions = me * tiles.shape[0] + lax.broadcasted_iota(jnp.int32, (128, tiles.shape[0]), 1)
+    kept = (mask_ref[...] == 1) | (positions == 0)
+    valid[...] = jnp.where(kept & (positions < count_ref[0]), 1.0, 0.0).T
 
     query_copy.wait()
     grad_copy.wait()
@@ -269,11 +288,13 @@
     value_grad[...] = jnp.zeros_like(value_grad)
     key_grad[...] = jnp.zeros_like(key_grad)
 
-    line_round(0, 1)
-    for distance in range(2, line):
-        line_round(0, distance)
-        if distance == 2:
-            open_round(1)
+    for distance in range(1, line):
+        own_round(0, distance)
+    other_round(0, 1)
+    side_round(0, line - 1)
+    open_own(1)
+    for distance in range(2, line - 1):
+        other_round(0, distance)
     close_round(0)
 
     tiles_copy.wait()
@@ -285,26 +306,33 @@
         key_parts[index] = part
         keys = keys - part.astype(jnp.float32)
 
-    line_round(1, 1)
-
-    @pl.loop(0, heads)
-    def _(head):
-        start = window(head)
-        cut = query_win[head]
-        scores = dot_nt(key_parts[2, :, pl.ds(start, WIN)], cut)
-        scores = scores + dot_nt(key_parts[1, :, pl.ds(start, WIN)], cut)
-        scores = scores + dot_nt(key_parts[0, :, pl.ds(start, WIN)], cut)
-        scores = jnp.where(valid_ref[...] > 0.0, scores * inv_scale, NEG_LARGE)
-        row_max = jnp.maximum(jnp.max(scores, axis=0, keepdims=True), NEG_FLOOR)
-        powers = jnp.exp(scores - row_max)
-        total = jnp.sum(powers, axis=0, keepdims=True)
-        expd[head] = powers
-        max_buf[pl.ds(head, 1), :] = row_max
-        lse_all[me, pl.ds(head, 1), :] = row_max + jnp.log(jnp.maximum(total, 1e-37))
-
+    def score(first, last):
+        @pl.loop(first, last, unroll=2)
+        def _(head):
+            start = window(head)
+            cut = query_win[head]
+            scores = dot_nt(key_parts[2, :, pl.ds(start, WIN)], cut)
+            scores = scores + dot_nt(key_parts[1, :, pl.ds(start, WIN)], cut)
+            scores = scores + dot_nt(key_parts[0, :, pl.ds(start, WIN)], cut)
+            scores = jnp.where(valid[:, :1] > 0.0, scores * inv_scale, NEG_LARGE)
+            row_max = jnp.maximum(jnp.max(scores, axis=0, keepdims=True), NEG_FLOOR)
+            powers = jnp.exp(scores - row_max)
+            total = jnp.sum(powers, axis=0, keepdims=True)
+            expd[head] = powers
+            max_buf[pl.ds(head, 1), :] = row_max
+            lse_all[me, pl.ds(head, 1), :] = row_max + jnp.log(jnp.maximum(total, 1e-37))
+
+    cuts = [heads * step // 4 for step in range(5)]
+    score(cuts[0], cuts[1])
+    own_round(1, 1)
+    score(cuts[1], cuts[2])
+    own_round(1, 2)
+    score(cuts[2], cuts[4])
     lse_copies = spread(lse_all, lse_send, lse_recv)
-    for distance in range(2, line):
-        line_round(1, distance)
+    for distance in range(3, line):
+        own_round(1, distance)
+    other_round(1, 1)
+    side_round(1, line - 1)
     collect(lse_all, lse_send, lse_recv)
     top = lse_all[0]
     for index in range(1, n_tile):
@@ -314,20 +342,20 @@
         total = total + jnp.exp(lse_all[index] - top)
     row_buf[...] = jnp.exp(max_buf[...] - (top + jnp.log(total)))
 
-    @pl.loop(0, heads)
-    def _(head):
-        expd[head] = expd[head] * row_buf[pl.ds(head, 1), :]
-
-    @pl.loop(0, heads)
+    @pl.loop(0, heads, unroll=2)
     def _(head):
         start = window(head)
-        value_grad[:, pl.ds(start, WIN)] += dot_nn(expd[head].astype(jnp.bfloat16), grad_win[head])
-
+        probs = expd[head] * row_buf[pl.ds(head, 1), :]
+        expd[head] = probs
+        value_grad[:, pl.ds(start, WIN)] += dot_nn(probs.astype(jnp.bfloat16), grad_win[head])
+
+    for distance in range(2, line - 1):
+        other_round(1, distance)
     close_round(1)
 
     values[...] = dot_nn(tiles[...], weights[1]).astype(jnp.bfloat16)
 
-    @pl.loop(0, heads)
+    @pl.loop(0, heads, unroll=2)
     def _(head):
         start = window(head)
         part = dot_nt(values[:, pl.ds(start, WIN)], grad_win[head])
@@ -338,7 +366,7 @@
 
     value_cast = value_grad[...].astype(jnp.bfloat16)
 
-    @pl.loop(0, 2 * chunks)
+    @pl.loop(0, 2 * chunks, unroll=2)
     def _(index):
         rows = pl.ds(pl.multiple_of(index * WIN, WIN), WIN)
         acc[index] = dot_nt(value_cast, weights[1, rows, :])
@@ -349,7 +377,7 @@
         delta = delta + weighted_all[index]
     row_buf[...] = delta
 
-    @pl.loop(0, heads)
+    @pl.loop(0, heads, unroll=2)
     def _(head):
         start = window(head)
         gap = prob_grad[head] - row_buf[pl.ds(head, 1), :]
@@ -359,42 +387,38 @@
     key_cast = key_grad[...].astype(jnp.bfloat16)
 
     def pair_copy(index):
+        columns = pl.ds(index * WIN, WIN)
         return pltpu.make_async_remote_copy(
-            src_ref=to_pair.at[index],
-            dst_ref=from_pair.at[index],
+            src_ref=to_pair.at[:, columns],
+            dst_ref=pair_ref.at[:, columns],
             send_sem=pair_send.at[index],
             recv_sem=pair_recv.at[index],
             device_id={"head": 1 - group},
             device_id_type=MESH,
         )
 
-    @pl.loop(0, chunks)
-    def _(index):
-        chunk = chunks * (1 - group) + index
+    def partial_sum(chunk):
         rows = pl.ds(pl.multiple_of(chunk * WIN, WIN), WIN)
-        to_pair[index] = (acc[chunk] + dot_nt(key_cast, weights[0, rows, :])).astype(jnp.bfloat16)
+        return (acc[chunk] + dot_nt(key_cast, weights[0, rows, :])).astype(jnp.bfloat16)
+
+    for index in range(chunks):
+        to_pair[:, index * WIN : (index + 1) * WIN] = partial_sum(chunks * (1 - group) + index)
         pair_copy(index).start()
-
-    @pl.loop(0, chunks)
-    def _(index):
-        chunk = chunks * group + index
-        rows = pl.ds(pl.multiple_of(chunk * WIN, WIN), WIN)
-        acc[chunk] += dot_nt(key_cast, weights[0, rows, :])
+    for index in range(chunks):
+        own_ref[:, index * WIN : (index + 1) * WIN] = partial_sum(chunks * group + index)
 
     for index in range(chunks):
         pair_copy(index).wait_recv()
-        total = acc[chunks * group + index] + from_pair[index].astype(jnp.float32)
-        out_ref[0, :, index * WIN : (index + 1) * WIN] = total.astype(jnp.bfloat16)
-
     for index in range(chunks):
         pair_copy(index).wait_send()
     for copy in lse_copies + sum_copies:
         copy.wait_send()
-    for cond, what in started:
+    assert len(started) <= SENDS
+    for index, (cond, what) in enumerate(started):
         if cond is None:
-            piece(*what).wait_send()
+            remote(index, *what).wait_send()
         else:
-            pl.when(cond)(functools.partial(lambda w: piece(*w).wait_send(), what))
+            pl.when(cond)(functools.partial(lambda i, w: remote(i, *w).wait_send(), index, what))
 
 
 def fused_device(across, tiles_in, key_weight, value_weight, queries, out_grad, valid_count, tile_mask):
@@ -404,17 +428,14 @@
     shard = key_weight.shape[0]
     heads = width // HDIM
     chunks = depth // 2 // WIN
-    positions = lax.axis_index("tile") * tile_dev + jnp.arange(tile_dev, dtype=jnp.int32)
-    kept = (tile_mask[0] == 1) | (positions == 0)
-    valid = ((positions < valid_count[0]) & kept).astype(jnp.float32)[:, None]
     bf16, f32 = jnp.bfloat16, jnp.float32
     dma = pltpu.SemaphoreType.DMA
-    return pl.pallas_call(
+    own, pair = pl.pallas_call(
         functools.partial(fused, n_tile // across, across, shard, width, heads, chunks),
-        out_shape=jax.ShapeDtypeStruct((1, tile_dev, depth // 2), bf16),
+        out_shape=[jax.ShapeDtypeStruct((tile_dev, depth // 2), bf16)] * 2,
         in_specs=[pl.BlockSpec(memory_space=pl.ANY)] * 5
-        + [pl.BlockSpec(memory_space=pltpu.VMEM)],
-        out_specs=pl.BlockSpec(memory_space=pltpu.VMEM),
+        + [pl.BlockSpec(memory_space=pltpu.SMEM), pl.BlockSpec(memory_space=pltpu.VMEM)],
+        out_specs=[pl.BlockSpec(memory_space=pltpu.VMEM)] * 2,
         scratch_shapes=[
             pltpu.VMEM((2, depth, width), bf16),
             pltpu.VMEM((tile_dev, depth), bf16),
@@ -433,11 +454,11 @@
             pltpu.VMEM((tile_dev, width), f32),
             pltpu.VMEM((tile_dev, width), f32),
             pltpu.VMEM((2 * chunks, tile_dev, WIN), f32),
-            pltpu.VMEM((chunks, tile_dev, WIN), bf16),
-            pltpu.VMEM((chunks, tile_dev, WIN), bf16),
+            pltpu.VMEM((tile_dev, chunks * WIN), bf16),
+            pltpu.VMEM((tile_dev, 128), f32),
             dma((5,)),
-            dma((2 * n_tile * 2 * 4,)),
-            dma((2 * n_tile * 2,)),
+            dma((SENDS,)),
+            dma((2 * n_tile * 2 * SUBS,)),
             dma((n_tile,)),
             dma((n_tile,)),
             dma((n_tile,)),
@@ -451,7 +472,8 @@
         cost_estimate=pl.CostEstimate(
             flops=4 * tile_dev * depth * width * 2, bytes_accessed=8 * 2**20, transcendentals=2**20
         ),
-    )(tiles_in, key_weight, value_weight, queries, out_grad, valid)
+    )(tiles_in, key_weight, value_weight, queries, out_grad, valid_count, tile_mask)
+    return (own.astype(f32) + pair.astype(f32)).astype(bf16)[None]
 
 
 def solution(mesh):
@@ -462,7 +484,7 @@
             across == 2
             and mesh.shape["head"] == 2
             and mesh.shape["tile"] >= 3 * across
-            and key_weight.shape[0] % 32 == 0
+            and key_weight.shape[0] % (32 * SUBS) == 0
             and tiles_in.shape[2] % (2 * WIN) == 0
         )
         body = functools.partial(fused_device, across) if fits else per_device

time: 90.2 us -> 76.3 us (0.85)
  Pallas kernels: 85.8 us -> 73.2 us
  local copies, waits for them, and re-layouts: 2.14 us -> 0 us
    pallas_call x1, Pallas kernels: 85.8 us -> 73.2 us  [fused_device(): pl.pallas_call(functools.partial(fused, n_tile // across, across, shard,...]
    broadcast_in_dim x0 -> x1, other arithmetic: none -> 2.27 us  [fused_device(): return (own.astype(f32) + pair.astype(f32)).astype(bf16)[None]]
    unnamed x1 -> x0, local copies, waits for them, and re-layouts: 1.97 us -> none
where the time goes in v2:
time: 76.3 us; the launch traced here: 76.2 us
  Pallas kernels  73.2 us (96%)
  other arithmetic  2.27 us (3%)
    pallas_call x1, Pallas kernels, fused_device(): pl.pallas_call(functools.partial(fused, n_tile // across, across, shard,...  73.2 us
    broadcast_in_dim x1, other arithmetic, fused_device(): return (own.astype(f32) + pair.astype(f32)).astype(bf16)[None]  2.27 us

profile of v2, /device:TPU:0, one launch (start us, length us, event | category | flops | bytes accessed | tf_op | source)
XLA Modules:
  0.0 76.2 jit_solution(687518147548844661)
XLA Ops:
  0.7 73.2 %shard_map.73 = (bf16[256,1280]{1,0:T(8,128)(2,1)}, bf16[256,1280]{1,0:T(8,128)(2,1)}) custom-call(bf16[1,256,2560]{2,1,0:T(8,128)(2,1)} %tiles_hbm.1, bf16[320,640]{1,0:T(8,128)(2,1)} %key_hbm.1, bf16[320,640]{1,0:T(8,128)(2,1)} %value_hbm.1, bf16[512,640]{1,0:T(8,128)(2,1)} %query_hbm.1, bf16[1,512,640]{2,1,0:T(8,128)(2,1)} %grad_hbm.1, ...), custom_call_target="tpu_custom_call" | custom-call | flops 3355443200 | bytes 8388608 | tf_op jit(solution)/shard_map/pallas_call | solution.py:433
  73.9 2.3 %fusion = bf16[1,256,1280]{2,1,0:T(8,128)(2,1)} fusion(bf16[256,1280]{1,0:T(8,128)(2,1)} %get-tuple-element.8, bf16[256,1280]{1,0:T(8,128)(2,1)} %get-tuple-element.7), kind=kLoop, calls=%fused_computation.1 | loop fusion | flops 1310720 | bytes 1966080 | tf_op jit(solution)/shard_map/broadcast_in_dim | solution.py:476

commit v3 on v2

--- a/solution.py
+++ b/solution.py
@@ -14,7 +14,7 @@
 NEG_FLOOR = -1e29
 WIN = 256
 SUBS = 2
-SENDS = 192
+SENDS = 256
 UP, DOWN, ACROSS, TWIN = range(4)
 MESH = pl.DeviceIdType.MESH
 
@@ -106,7 +106,13 @@
 ):
     n_tile = line * across
     half = shard // 2
-    size = half // SUBS
+    bounds = list(range(0, width, WIN)) + [width]
+    cuts_of = [(0, 0, width, SUBS)] + [(1, a, b - a, 1) for a, b in zip(bounds, bounds[1:])]
+    members = [
+        [head for head in range(heads) if a < (head + 1) * HDIM <= b]
+        for a, b in zip(bounds, bounds[1:])
+    ]
+    groups = len(members)
     inv_scale = HDIM ** (-0.5)
     me = lax.axis_index("tile")
     slide = lax.axis_index("dp")
@@ -145,13 +151,21 @@
     pl.semaphore_signal(barrier, inc=1, device_id={"head": 1 - group}, device_id_type=MESH)
     pl.semaphore_wait(barrier, n_tile + 1)
 
+    def subs(m):
+        return range(cuts_of[m][3])
+
     def piece(m, owner, part, sub, way, first=False):
+        which, column, columns, count = cuts_of[m]
+        size = half // count
         offset = part * half + sub * size
+        cols = pl.ds(column, columns)
         rows = pl.ds(pl.multiple_of(owner * shard + offset, 16), size)
-        src = weights.at[m, rows]
+        src = weights.at[which, rows, cols]
         if first:
-            src = sources[m].at[pl.ds(pl.multiple_of(offset, 16), size)]
-        return src, weights.at[m, rows], ((m * n_tile + owner) * 2 + part) * SUBS + sub, devices[way]
+            src = sources[which].at[pl.ds(pl.multiple_of(offset, 16), size), cols]
+        base = n_tile * 2 * sum(cut[3] for cut in cuts_of[:m])
+        landing = base + (owner * 2 + part) * count + sub
+        return src, weights.at[which, rows, cols], landing, devices[way]
 
     def remote(index, *what):
         src, dst, landing, device = piece(*what)
@@ -193,20 +207,20 @@
         ]
 
     def open_own(m):
-        for sub in range(SUBS):
+        for sub in subs(m):
             for way, can in ways:
                 send(can, m, me, mine, sub, way, True)
             send(None, m, me, mine, sub, ACROSS, True)
 
     def side_round(m, distance):
-        for sub in range(SUBS):
+        for sub in subs(m):
             for there, owner in held_at(beside, distance):
                 arrive(there, m, owner, mine, sub)
                 send(there, m, owner, mine, sub, TWIN)
 
     def own_round(m, distance):
         last = distance == line - 1
-        for sub in range(SUBS):
+        for sub in subs(m):
             for (there, owner), (way, can) in zip(held_at(me, distance), ways):
                 arrive(there, m, owner, mine, sub)
                 if not last:
@@ -216,19 +230,19 @@
                     send(there, m, owner, mine, sub, TWIN)
         for way, can, ends in ((UP, can_up, z), (DOWN, can_down, line - 1 - z)):
             turn = jnp.maximum(ends, 1) == distance
-            for sub in range(SUBS):
+            for sub in subs(m) if not last else ():
                 send(both(turn, can), m, me, other, sub, way, True)
         side_round(m, distance - 1)
 
     def other_round(m, distance):
-        for sub in range(SUBS):
+        for sub in subs(m):
             for (there, owner), (way, can) in zip(held_at(me, distance), ways):
                 arrive(there, m, owner, other, sub)
                 if distance + 1 < line - 1:
                     send(both(there, can), m, owner, other, sub, way)
 
     def close_round(m):
-        for sub in range(SUBS):
+        for sub in subs(m):
             for distance in range(line):
                 for there, owner in held_at(beside, distance):
                     arrive(there, m, owner, other, sub)
@@ -287,6 +301,8 @@
 
     value_grad[...] = jnp.zeros_like(value_grad)
     key_grad[...] = jnp.zeros_like(key_grad)
+    values[...] = jnp.zeros_like(values)
+    weighted_all[:, me] = jnp.zeros((groups,) + weighted_all.shape[2:], jnp.float32)
 
     for distance in range(1, line):
         own_round(0, distance)
@@ -322,6 +338,52 @@
             max_buf[pl.ds(head, 1), :] = row_max
             lse_all[me, pl.ds(head, 1), :] = row_max + jnp.log(jnp.maximum(total, 1e-37))
 
+    def others(m):
+        for distance in range(2, line - 1):
+            other_round(m, distance)
+
+    def late_rounds(m):
+        for distance in range(3, line):
+            own_round(m, distance)
+        other_round(m, 1)
+        side_round(m, line - 1)
+
+    def normalise(first, last):
+        @pl.loop(first, last, unroll=2)
+        def _(head):
+            start = window(head)
+            probs = expd[head] * row_buf[pl.ds(head, 1), :]
+            expd[head] = probs
+            value_grad[:, pl.ds(start, WIN)] += dot_nn(probs.astype(jnp.bfloat16), grad_win[head])
+
+    def fixed(head):
+        start = 128 * min((head * HDIM) // 128, (width - WIN) // 128)
+        return slice(start, start + WIN)
+
+    def weigh(group_index):
+        cols = slice(bounds[group_index], bounds[group_index + 1])
+        values[:, cols] = dot_nn(tiles[...], weights[1, :, cols]).astype(jnp.bfloat16)
+        for head in members[group_index]:
+            part = dot_nt(values[:, fixed(head)], grad_win[head])
+            prob_grad[head] = part
+            weighted_all[group_index, me, head : head + 1, :] = jnp.sum(
+                expd[head] * part, axis=0, keepdims=True
+            )
+        return spread(
+            weighted_all.at[group_index], sum_send.at[group_index], sum_recv.at[group_index]
+        )
+
+    def differentiate(group_index):
+        collect(weighted_all.at[group_index], sum_send.at[group_index], sum_recv.at[group_index])
+        delta = weighted_all[group_index, 0]
+        for index in range(1, n_tile):
+            delta = delta + weighted_all[group_index, index]
+        row_buf[...] = delta
+        for head in members[group_index]:
+            gap = prob_grad[head] - row_buf[head : head + 1, :]
+            dscore = (inv_scale * expd[head] * gap).astype(jnp.bfloat16)
+            key_grad[:, fixed(head)] += dot_nn(dscore, query_win[head])
+
     cuts = [heads * step // 4 for step in range(5)]
     score(cuts[0], cuts[1])
     own_round(1, 1)
@@ -329,10 +391,8 @@
     own_round(1, 2)
     score(cuts[2], cuts[4])
     lse_copies = spread(lse_all, lse_send, lse_recv)
-    for distance in range(3, line):
-        own_round(1, distance)
-    other_round(1, 1)
-    side_round(1, line - 1)
+    late_rounds(1)
+    open_own(2)
     collect(lse_all, lse_send, lse_recv)
     top = lse_all[0]
     for index in range(1, n_tile):
@@ -342,49 +402,39 @@
         total = total + jnp.exp(lse_all[index] - top)
     row_buf[...] = jnp.exp(max_buf[...] - (top + jnp.log(total)))
 
-    @pl.loop(0, heads, unroll=2)
-    def _(head):
-        start = window(head)
-        probs = expd[head] * row_buf[pl.ds(head, 1), :]
-        expd[head] = probs
-        value_grad[:, pl.ds(start, WIN)] += dot_nn(probs.astype(jnp.bfloat16), grad_win[head])
-
-    for distance in range(2, line - 1):
-        other_round(1, distance)
-    close_round(1)
-
-    values[...] = dot_nn(tiles[...], weights[1]).astype(jnp.bfloat16)
-
-    @pl.loop(0, heads, unroll=2)
-    def _(head):
-        start = window(head)
-        part = dot_nt(values[:, pl.ds(start, WIN)], grad_win[head])
-        prob_grad[head] = part
-        weighted_all[me, pl.ds(head, 1), :] = jnp.sum(expd[head] * part, axis=0, keepdims=True)
-
-    sum_copies = spread(weighted_all, sum_send, sum_recv)
+    others(1)
+    own_round(2, 1)
+    normalise(cuts[0], cuts[2])
+    own_round(2, 2)
+    normalise(cuts[2], cuts[4])
+    sum_copies = []
+    for index in range(groups):
+        m = index + 1
+        close_round(m)
+        sum_copies += weigh(index)
+        if index + 1 < groups:
+            if index > 0:
+                own_round(m + 1, 2)
+            late_rounds(m + 1)
+            if index + 2 < groups:
+                open_own(m + 2)
+            differentiate(index)
+            others(m + 1)
+            if index + 2 < groups:
+                own_round(m + 2, 1)
 
     value_cast = value_grad[...].astype(jnp.bfloat16)
+    ready = members[-1][0] * HDIM // 128 * 128
+    early_cast = key_grad[:, :ready].astype(jnp.bfloat16)
 
     @pl.loop(0, 2 * chunks, unroll=2)
     def _(index):
         rows = pl.ds(pl.multiple_of(index * WIN, WIN), WIN)
-        acc[index] = dot_nt(value_cast, weights[1, rows, :])
-
-    collect(weighted_all, sum_send, sum_recv)
-    delta = weighted_all[0]
-    for index in range(1, n_tile):
-        delta = delta + weighted_all[index]
-    row_buf[...] = delta
-
-    @pl.loop(0, heads, unroll=2)
-    def _(head):
-        start = window(head)
-        gap = prob_grad[head] - row_buf[pl.ds(head, 1), :]
-        dscore = (inv_scale * expd[head] * gap).astype(jnp.bfloat16)
-        key_grad[:, pl.ds(start, WIN)] += dot_nn(dscore, query_win[head])
-
-    key_cast = key_grad[...].astype(jnp.bfloat16)
+        part = dot_nt(value_cast, weights[1, rows, :])
+        acc[index] = part + dot_nt(early_cast, weights[0, rows, :ready])
+
+    differentiate(groups - 1)
+    key_cast = key_grad[:, ready:].astype(jnp.bfloat16)
 
     def pair_copy(index):
         columns = pl.ds(index * WIN, WIN)
@@ -399,7 +449,7 @@
 
     def partial_sum(chunk):
         rows = pl.ds(pl.multiple_of(chunk * WIN, WIN), WIN)
-        return (acc[chunk] + dot_nt(key_cast, weights[0, rows, :])).astype(jnp.bfloat16)
+        return (acc[chunk] + dot_nt(key_cast, weights[0, rows, ready:])).astype(jnp.bfloat16)
 
     for index in range(chunks):
         to_pair[:, index * WIN : (index + 1) * WIN] = partial_sum(chunks * (1 - group) + index)
@@ -428,6 +478,7 @@
     shard = key_weight.shape[0]
     heads = width // HDIM
     chunks = depth // 2 // WIN
+    groups = pl.cdiv(width, WIN)
     bf16, f32 = jnp.bfloat16, jnp.float32
     dma = pltpu.SemaphoreType.DMA
     own, pair = pl.pallas_call(
@@ -449,7 +500,7 @@
             pltpu.VMEM((heads, tile_dev, latents), f32),
             pltpu.VMEM((heads, latents), f32),
             pltpu.VMEM((n_tile, heads, latents), f32),
-            pltpu.VMEM((n_tile, heads, latents), f32),
+            pltpu.VMEM((groups, n_tile, heads, latents), f32),
             pltpu.VMEM((heads, latents), f32),
             pltpu.VMEM((tile_dev, width), f32),
             pltpu.VMEM((tile_dev, width), f32),
@@ -458,11 +509,11 @@
             pltpu.VMEM((tile_dev, 128), f32),
             dma((5,)),
             dma((SENDS,)),
-            dma((2 * n_tile * 2 * SUBS,)),
+            dma((n_tile * 2 * (SUBS + groups),)),
             dma((n_tile,)),
             dma((n_tile,)),
-            dma((n_tile,)),
-            dma((n_tile,)),
+            dma((groups, n_tile)),
+            dma((groups, n_tile)),
             dma((chunks,)),
             dma((chunks,)),
         ],

time: 76.3 us -> 93.8 us (1.23)
  Pallas kernels: 73.2 us -> 90.7 us
    pallas_call x1, Pallas kernels: 73.2 us -> 90.7 us  [fused_device(): pl.pallas_call(functools.partial(fused, n_tile // across, across, shard,...]
where the time goes in v3:
time: 93.8 us; the launch traced here: 93.7 us
  Pallas kernels  90.7 us (97%)
  other arithmetic  2.27 us (2%)
    pallas_call x1, Pallas kernels, fused_device(): pl.pallas_call(functools.partial(fused, n_tile // across, across, shard,...  90.7 us
    broadcast_in_dim x1, other arithmetic, fused_device(): return (own.astype(f32) + pair.astype(f32)).astype(bf16)[None]  2.27 us

profile of v3, /device:TPU:0, one launch (start us, length us, event | category | flops | bytes accessed | tf_op | source)
XLA Modules:
  0.0 93.7 jit_solution(8681531574615720713)
XLA Ops:
  0.7 90.7 %shard_map.73 = (bf16[256,1280]{1,0:T(8,128)(2,1)}, bf16[256,1280]{1,0:T(8,128)(2,1)}) custom-call(bf16[1,256,2560]{2,1,0:T(8,128)(2,1)} %tiles_hbm.1, bf16[320,640]{1,0:T(8,128)(2,1)} %key_hbm.1, bf16[320,640]{1,0:T(8,128)(2,1)} %value_hbm.1, bf16[512,640]{1,0:T(8,128)(2,1)} %query_hbm.1, bf16[1,512,640]{2,1,0:T(8,128)(2,1)} %grad_hbm.1, ...), custom_call_target="tpu_custom_call" | custom-call | flops 3355443200 | bytes 8388608 | tf_op jit(solution)/shard_map/pallas_call | solution.py:484
  91.4 2.3 %fusion = bf16[1,256,1280]{2,1,0:T(8,128)(2,1)} fusion(bf16[256,1280]{1,0:T(8,128)(2,1)} %get-tuple-element.8, bf16[256,1280]{1,0:T(8,128)(2,1)} %get-tuple-element.7), kind=kLoop, calls=%fused_computation.1 | loop fusion | flops 1310720 | bytes 1966080 | tf_op jit(solution)/shard_map/broadcast_in_dim | solution.py:527

commit v4 on v2

--- a/solution.py
+++ b/solution.py
@@ -100,7 +100,7 @@
     line, across, shard, width, heads, chunks,
     tiles_hbm, key_hbm, value_hbm, query_hbm, grad_hbm, count_ref, mask_ref,
     own_ref, pair_ref,
-    weights, tiles, query, grad, query_win, grad_win, key_parts, values, expd, prob_grad,
+    weights, tiles, query, grad, query_win, grad_win, query_turn, grad_turn, key_parts, values, expd, prob_grad,
     max_buf, lse_all, weighted_all, row_buf, value_grad, key_grad, acc, to_pair, valid,
     local_sem, send_sem, recv_sem, lse_send, lse_recv, sum_send, sum_recv, pair_send, pair_recv,
 ):
@@ -196,6 +196,9 @@
         for sub in range(SUBS):
             for way, can in ways:
                 send(can, m, me, mine, sub, way, True)
+
+    def open_side(m):
+        for sub in range(SUBS):
             send(None, m, me, mine, sub, ACROSS, True)
 
     def side_round(m, distance):
@@ -239,6 +242,10 @@
         start = 128 * jnp.minimum((head * HDIM) // 128, (width - WIN) // 128)
         return pl.multiple_of(start, 128)
 
+    def fixed(head):
+        start = 128 * min((head * HDIM) // 128, (width - WIN) // 128)
+        return slice(start, start + WIN)
+
     def spread(buffer, send_sems, recv_sems):
         copies = []
         for step in range(1, n_tile):
@@ -268,6 +275,7 @@
             ).wait_recv()
 
     open_own(0)
+    open_side(0)
 
     positions = me * tiles.shape[0] + lax.broadcasted_iota(jnp.int32, (128, tiles.shape[0]), 1)
     kept = (mask_ref[...] == 1) | (positions == 0)
@@ -281,20 +289,23 @@
         start = window(head)
         column = start + lax.broadcasted_iota(jnp.int32, (query.shape[0], WIN), 1)
         inside = (column >= head * HDIM) & (column < (head + 1) * HDIM)
-        for whole, cut in ((query, query_win), (grad, grad_win)):
-            part = whole[:, pl.ds(start, WIN)].astype(jnp.float32)
-            cut[head] = jnp.where(inside, part, 0.0).astype(jnp.bfloat16)
+        for whole, cut, turn in ((query, query_win, query_turn), (grad, grad_win, grad_turn)):
+            part = jnp.where(inside, whole[:, pl.ds(start, WIN)].astype(jnp.float32), 0.0)
+            cut[head] = part.astype(jnp.bfloat16)
+            turn[head] = part.T.astype(jnp.bfloat16)
 
     value_grad[...] = jnp.zeros_like(value_grad)
     key_grad[...] = jnp.zeros_like(key_grad)
 
     for distance in range(1, line):
         own_round(0, distance)
+    open_side(1)
     other_round(0, 1)
+    open_own(1)
     side_round(0, line - 1)
-    open_own(1)
     for distance in range(2, line - 1):
         other_round(0, distance)
+    own_round(1, 1)
     close_round(0)
 
     tiles_copy.wait()
@@ -310,10 +321,10 @@
         @pl.loop(first, last, unroll=2)
         def _(head):
             start = window(head)
-            cut = query_win[head]
-            scores = dot_nt(key_parts[2, :, pl.ds(start, WIN)], cut)
-            scores = scores + dot_nt(key_parts[1, :, pl.ds(start, WIN)], cut)
-            scores = scores + dot_nt(key_parts[0, :, pl.ds(start, WIN)], cut)
+            cut = query_turn[head]
+            scores = dot_nn(key_parts[2, :, pl.ds(start, WIN)], cut)
+            scores = scores + dot_nn(key_parts[1, :, pl.ds(start, WIN)], cut)
+            scores = scores + dot_nn(key_parts[0, :, pl.ds(start, WIN)], cut)
             scores = jnp.where(valid[:, :1] > 0.0, scores * inv_scale, NEG_LARGE)
             row_max = jnp.maximum(jnp.max(scores, axis=0, keepdims=True), NEG_FLOOR)
             powers = jnp.exp(scores - row_max)
@@ -324,10 +335,8 @@
 
     cuts = [heads * step // 4 for step in range(5)]
     score(cuts[0], cuts[1])
-    own_round(1, 1)
-    score(cuts[1], cuts[2])
     own_round(1, 2)
-    score(cuts[2], cuts[4])
+    score(cuts[1], cuts[4])
     lse_copies = spread(lse_all, lse_send, lse_recv)
     for distance in range(3, line):
         own_round(1, distance)
@@ -355,12 +364,10 @@
 
     values[...] = dot_nn(tiles[...], weights[1]).astype(jnp.bfloat16)
 
-    @pl.loop(0, heads, unroll=2)
-    def _(head):
-        start = window(head)
-        part = dot_nt(values[:, pl.ds(start, WIN)], grad_win[head])
+    for head in range(heads):
+        part = dot_nn(values[:, fixed(head)], grad_turn[head])
         prob_grad[head] = part
-        weighted_all[me, pl.ds(head, 1), :] = jnp.sum(expd[head] * part, axis=0, keepdims=True)
+        weighted_all[me, head : head + 1, :] = jnp.sum(expd[head] * part, axis=0, keepdims=True)
 
     sum_copies = spread(weighted_all, sum_send, sum_recv)
 
@@ -377,12 +384,10 @@
         delta = delta + weighted_all[index]
     row_buf[...] = delta
 
-    @pl.loop(0, heads, unroll=2)
-    def _(head):
-        start = window(head)
-        gap = prob_grad[head] - row_buf[pl.ds(head, 1), :]
+    for head in range(heads):
+        gap = prob_grad[head] - row_buf[head : head + 1, :]
         dscore = (inv_scale * expd[head] * gap).astype(jnp.bfloat16)
-        key_grad[:, pl.ds(start, WIN)] += dot_nn(dscore, query_win[head])
+        key_grad[:, fixed(head)] += dot_nn(dscore, query_win[head])
 
     key_cast = key_grad[...].astype(jnp.bfloat16)
 
@@ -443,6 +448,8 @@
             pltpu.VMEM((latents, width), bf16),
             pltpu.VMEM((heads, latents, WIN), bf16),
             pltpu.VMEM((heads, latents, WIN), bf16),
+            pltpu.VMEM((heads, WIN, latents), bf16),
+            pltpu.VMEM((heads, WIN, latents), bf16),
             pltpu.VMEM((3, tile_dev, width), bf16),
             pltpu.VMEM((tile_dev, width), bf16),
             pltpu.VMEM((heads, tile_dev, latents), f32),

time: 76.3 us -> 74.7 us (0.979)
  Pallas kernels: 73.2 us -> 71.6 us
    pallas_call x1, Pallas kernels: 73.2 us -> 71.6 us  [fused_device(): pl.pallas_call(functools.partial(fused, n_tile // across, across, shard,...]
where the time goes in v4:
time: 74.7 us; the launch traced here: 74.5 us
  Pallas kernels  71.6 us (96%)
  other arithmetic  2.27 us (3%)
    pallas_call x1, Pallas kernels, fused_device(): pl.pallas_call(functools.partial(fused, n_tile // across, across, shard,...  71.6 us
    broadcast_in_dim x1, other arithmetic, fused_device(): return (own.astype(f32) + pair.astype(f32)).astype(bf16)[None]  2.27 us

profile of v4, /device:TPU:0, one launch (start us, length us, event | category | flops | bytes accessed | tf_op | source)
XLA Modules:
  0.0 74.5 jit_solution(17308266209737928696)
XLA Ops:
  0.7 71.6 %shard_map.73 = (bf16[256,1280]{1,0:T(8,128)(2,1)}, bf16[256,1280]{1,0:T(8,128)(2,1)}) custom-call(bf16[1,256,2560]{2,1,0:T(8,128)(2,1)} %tiles_hbm.1, bf16[320,640]{1,0:T(8,128)(2,1)} %key_hbm.1, bf16[320,640]{1,0:T(8,128)(2,1)} %value_hbm.1, bf16[512,640]{1,0:T(8,128)(2,1)} %query_hbm.1, bf16[1,512,640]{2,1,0:T(8,128)(2,1)} %grad_hbm.1, ...), custom_call_target="tpu_custom_call" | custom-call | flops 3355443200 | bytes 8388608 | tf_op jit(solution)/shard_map/pallas_call | solution.py:438
  72.2 2.3 %fusion = bf16[1,256,1280]{2,1,0:T(8,128)(2,1)} fusion(bf16[256,1280]{1,0:T(8,128)(2,1)} %get-tuple-element.8, bf16[256,1280]{1,0:T(8,128)(2,1)} %get-tuple-element.7), kind=kLoop, calls=%fused_computation.1 | loop fusion | flops 1310720 | bytes 1966080 | tf_op jit(solution)/shard_map/broadcast_in_dim | solution.py:483

commit v5 on v4

--- a/solution.py
+++ b/solution.py
@@ -205,7 +205,8 @@
         for sub in range(SUBS):
             for there, owner in held_at(beside, distance):
                 arrive(there, m, owner, mine, sub)
-                send(there, m, owner, mine, sub, TWIN)
+                if distance > 0:
+                    send(there, m, owner, mine, sub, TWIN)
 
     def own_round(m, distance):
         last = distance == line - 1
@@ -217,6 +218,9 @@
                 send(there, m, owner, mine, sub, ACROSS)
                 if last:
                     send(there, m, owner, mine, sub, TWIN)
+        if last:
+            for sub in range(SUBS):
+                send(None, m, me, other, sub, ACROSS, True)
         for way, can, ends in ((UP, can_up, z), (DOWN, can_down, line - 1 - z)):
             turn = jnp.maximum(ends, 1) == distance
             for sub in range(SUBS):

time: 74.7 us -> 72.8 us (0.975)
  Pallas kernels: 71.6 us -> 69.7 us
    pallas_call x1, Pallas kernels: 71.6 us -> 69.7 us  [fused_device(): pl.pallas_call(functools.partial(fused, n_tile // across, across, shard,...]
where the time goes in v5:
time: 72.8 us; the launch traced here: 72.6 us
  Pallas kernels  69.7 us (96%)
  other arithmetic  2.27 us (3%)
    pallas_call x1, Pallas kernels, fused_device(): pl.pallas_call(functools.partial(fused, n_tile // across, across, shard,...  69.7 us
    broadcast_in_dim x1, other arithmetic, fused_device(): return (own.astype(f32) + pair.astype(f32)).astype(bf16)[None]  2.27 us

profile of v5, /device:TPU:0, one launch (start us, length us, event | category | flops | bytes accessed | tf_op | source)
XLA Modules:
  0.0 72.6 jit_solution(17928342102849518204)
XLA Ops:
  0.7 69.7 %shard_map.73 = (bf16[256,1280]{1,0:T(8,128)(2,1)}, bf16[256,1280]{1,0:T(8,128)(2,1)}) custom-call(bf16[1,256,2560]{2,1,0:T(8,128)(2,1)} %tiles_hbm.1, bf16[320,640]{1,0:T(8,128)(2,1)} %key_hbm.1, bf16[320,640]{1,0:T(8,128)(2,1)} %value_hbm.1, bf16[512,640]{1,0:T(8,128)(2,1)} %query_hbm.1, bf16[1,512,640]{2,1,0:T(8,128)(2,1)} %grad_hbm.1, ...), custom_call_target="tpu_custom_call" | custom-call | flops 3355443200 | bytes 8388608 | tf_op jit(solution)/shard_map/pallas_call | solution.py:442
  70.3 2.3 %fusion = bf16[1,256,1280]{2,1,0:T(8,128)(2,1)} fusion(bf16[256,1280]{1,0:T(8,128)(2,1)} %get-tuple-element.8, bf16[256,1280]{1,0:T(8,128)(2,1)} %get-tuple-element.7), kind=kLoop, calls=%fused_computation.1 | loop fusion | flops 1310720 | bytes 1966080 | tf_op jit(solution)/shard_map/broadcast_in_dim | solution.py:487

commit v6 on v5

--- a/solution.py
+++ b/solution.py
@@ -13,7 +13,7 @@
 NEG_LARGE = -1e30
 NEG_FLOOR = -1e29
 WIN = 256
-SUBS = 2
+SUBS = 1
 SENDS = 192
 UP, DOWN, ACROSS, TWIN = range(4)
 MESH = pl.DeviceIdType.MESH

time: 72.8 us -> 78.9 us (1.084)
  Pallas kernels: 69.7 us -> 75.8 us
    pallas_call x1, Pallas kernels: 69.7 us -> 75.8 us  [fused_device(): pl.pallas_call(functools.partial(fused, n_tile // across, across, shard,...]
where the time goes in v6:
time: 78.9 us; the launch traced here: 78.8 us
  Pallas kernels  75.8 us (96%)
  other arithmetic  2.27 us (3%)
    pallas_call x1, Pallas kernels, fused_device(): pl.pallas_call(functools.partial(fused, n_tile // across, across, shard,...  75.8 us
    broadcast_in_dim x1, other arithmetic, fused_device(): return (own.astype(f32) + pair.astype(f32)).astype(bf16)[None]  2.27 us

profile of v6, /device:TPU:0, one launch (start us, length us, event | category | flops | bytes accessed | tf_op | source)
XLA Modules:
  0.0 78.8 jit_solution(9627505180995610617)
XLA Ops:
  0.7 75.8 %shard_map.73 = (bf16[256,1280]{1,0:T(8,128)(2,1)}, bf16[256,1280]{1,0:T(8,128)(2,1)}) custom-call(bf16[1,256,2560]{2,1,0:T(8,128)(2,1)} %tiles_hbm.1, bf16[320,640]{1,0:T(8,128)(2,1)} %key_hbm.1, bf16[320,640]{1,0:T(8,128)(2,1)} %value_hbm.1, bf16[512,640]{1,0:T(8,128)(2,1)} %query_hbm.1, bf16[1,512,640]{2,1,0:T(8,128)(2,1)} %grad_hbm.1, ...), custom_call_target="tpu_custom_call" | custom-call | flops 3355443200 | bytes 8388608 | tf_op jit(solution)/shard_map/pallas_call | solution.py:442
  76.5 2.3 %fusion = bf16[1,256,1280]{2,1,0:T(8,128)(2,1)} fusion(bf16[256,1280]{1,0:T(8,128)(2,1)} %get-tuple-element.8, bf16[256,1280]{1,0:T(8,128)(2,1)} %get-tuple-element.7), kind=kLoop, calls=%fused_computation.1 | loop fusion | flops 1310720 | bytes 1966080 | tf_op jit(solution)/shard_map/broadcast_in_dim | solution.py:487

commit v7 on v6

--- a/solution.py
+++ b/solution.py
@@ -13,8 +13,8 @@
 NEG_LARGE = -1e30
 NEG_FLOOR = -1e29
 WIN = 256
-SUBS = 1
-SENDS = 192
+SUBS = 5
+SENDS = 512
 UP, DOWN, ACROSS, TWIN = range(4)
 MESH = pl.DeviceIdType.MESH
 
@@ -178,6 +178,16 @@
         else:
             pl.when(cond)(lambda: remote(0, m, owner, part, sub, ACROSS).wait_recv())
 
+    def drain(m):
+        assert len(started) <= SENDS
+        for index, (cond, what) in enumerate(started):
+            if what[0] != m:
+                continue
+            if cond is None:
+                remote(index, *what).wait_send()
+            else:
+                pl.when(cond)(functools.partial(lambda i, w: remote(i, *w).wait_send(), index, what))
+
     def both(a, b):
         return b if a is None else (a if b is None else jnp.logical_and(a, b))
 
@@ -364,6 +374,7 @@
 
     for distance in range(2, line - 1):
         other_round(1, distance)
+    drain(0)
     close_round(1)
 
     values[...] = dot_nn(tiles[...], weights[1]).astype(jnp.bfloat16)
@@ -374,6 +385,7 @@
         weighted_all[me, head : head + 1, :] = jnp.sum(expd[head] * part, axis=0, keepdims=True)
 
     sum_copies = spread(weighted_all, sum_send, sum_recv)
+    drain(1)
 
     value_cast = value_grad[...].astype(jnp.bfloat16)
 
@@ -422,12 +434,6 @@
         pair_copy(index).wait_send()
     for copy in lse_copies + sum_copies:
         copy.wait_send()
-    assert len(started) <= SENDS
-    for index, (cond, what) in enumerate(started):
-        if cond is None:
-            remote(index, *what).wait_send()
-        else:
-            pl.when(cond)(functools.partial(lambda i, w: remote(i, *w).wait_send(), index, what))
 
 
 def fused_device(across, tiles_in, key_weight, value_weight, queries, out_grad, valid_count, tile_mask):

time: 78.9 us -> 77 us (0.976)
  Pallas kernels: 75.8 us -> 73.9 us
    pallas_call x1, Pallas kernels: 75.8 us -> 73.9 us  [fused_device(): pl.pallas_call(functools.partial(fused, n_tile // across, across, shard,...]
where the time goes in v7:
time: 77 us; the launch traced here: 76.9 us
  Pallas kernels  73.9 us (96%)
  other arithmetic  2.27 us (3%)
    pallas_call x1, Pallas kernels, fused_device(): pl.pallas_call(functools.partial(fused, n_tile // across, across, shard,...  73.9 us
    broadcast_in_dim x1, other arithmetic, fused_device(): return (own.astype(f32) + pair.astype(f32)).astype(bf16)[None]  2.27 us

profile of v7, /device:TPU:0, one launch (start us, length us, event | category | flops | bytes accessed | tf_op | source)
XLA Modules:
  0.0 76.9 jit_solution(1422671345038294474)
XLA Ops:
  0.7 73.9 %shard_map.73 = (bf16[256,1280]{1,0:T(8,128)(2,1)}, bf16[256,1280]{1,0:T(8,128)(2,1)}) custom-call(bf16[1,256,2560]{2,1,0:T(8,128)(2,1)} %tiles_hbm.1, bf16[320,640]{1,0:T(8,128)(2,1)} %key_hbm.1, bf16[320,640]{1,0:T(8,128)(2,1)} %value_hbm.1, bf16[512,640]{1,0:T(8,128)(2,1)} %query_hbm.1, bf16[1,512,640]{2,1,0:T(8,128)(2,1)} %grad_hbm.1, ...), custom_call_target="tpu_custom_call" | custom-call | flops 3355443200 | bytes 8388608 | tf_op jit(solution)/shard_map/pallas_call | solution.py:448
  74.6 2.3 %fusion = bf16[1,256,1280]{2,1,0:T(8,128)(2,1)} fusion(bf16[256,1280]{1,0:T(8,128)(2,1)} %get-tuple-element.8, bf16[256,1280]{1,0:T(8,128)(2,1)} %get-tuple-element.7), kind=kLoop, calls=%fused_computation.1 | loop fusion | flops 1310720 | bytes 1966080 | tf_op jit(solution)/shard_map/broadcast_in_dim | solution.py:493

commit v8 on v7

--- a/solution.py
+++ b/solution.py
@@ -13,8 +13,8 @@
 NEG_LARGE = -1e30
 NEG_FLOOR = -1e29
 WIN = 256
-SUBS = 5
-SENDS = 512
+SUBS = 2
+SENDS = 192
 UP, DOWN, ACROSS, TWIN = range(4)
 MESH = pl.DeviceIdType.MESH
 
@@ -350,10 +350,11 @@
     cuts = [heads * step // 4 for step in range(5)]
     score(cuts[0], cuts[1])
     own_round(1, 2)
-    score(cuts[1], cuts[4])
-    lse_copies = spread(lse_all, lse_send, lse_recv)
+    score(cuts[1], cuts[2])
     for distance in range(3, line):
         own_round(1, distance)
+    score(cuts[2], cuts[4])
+    lse_copies = spread(lse_all, lse_send, lse_recv)
     other_round(1, 1)
     side_round(1, line - 1)
     collect(lse_all, lse_send, lse_recv)

time: 77 us -> 74 us (0.961)
  Pallas kernels: 73.9 us -> 70.9 us
    pallas_call x1, Pallas kernels: 73.9 us -> 70.9 us  [fused_device(): pl.pallas_call(functools.partial(fused, n_tile // across, across, shard,...]
where the time goes in v8:
time: 74 us; the launch traced here: 73.8 us
  Pallas kernels  70.9 us (96%)
  other arithmetic  2.27 us (3%)
    pallas_call x1, Pallas kernels, fused_device(): pl.pallas_call(functools.partial(fused, n_tile // across, across, shard,...  70.9 us
    broadcast_in_dim x1, other arithmetic, fused_device(): return (own.astype(f32) + pair.astype(f32)).astype(bf16)[None]  2.27 us

profile of v8, /device:TPU:0, one launch (start us, length us, event | category | flops | bytes accessed | tf_op | source)
XLA Modules:
  0.0 73.8 jit_solution(3512279714991747201)
XLA Ops:
  0.7 70.9 %shard_map.73 = (bf16[256,1280]{1,0:T(8,128)(2,1)}, bf16[256,1280]{1,0:T(8,128)(2,1)}) custom-call(bf16[1,256,2560]{2,1,0:T(8,128)(2,1)} %tiles_hbm.1, bf16[320,640]{1,0:T(8,128)(2,1)} %key_hbm.1, bf16[320,640]{1,0:T(8,128)(2,1)} %value_hbm.1, bf16[512,640]{1,0:T(8,128)(2,1)} %query_hbm.1, bf16[1,512,640]{2,1,0:T(8,128)(2,1)} %grad_hbm.1, ...), custom_call_target="tpu_custom_call" | custom-call | flops 3355443200 | bytes 8388608 | tf_op jit(solution)/shard_map/pallas_call | solution.py:449
  71.6 2.3 %fusion = bf16[1,256,1280]{2,1,0:T(8,128)(2,1)} fusion(bf16[256,1280]{1,0:T(8,128)(2,1)} %get-tuple-element.8, bf16[256,1280]{1,0:T(8,128)(2,1)} %get-tuple-element.7), kind=kLoop, calls=%fused_computation.1 | loop fusion | flops 1310720 | bytes 1966080 | tf_op jit(solution)/shard_map/broadcast_in_dim | solution.py:494
